TPU v7x, 32 devices: a whole 2x2x4 slice. The times are simulated.
32 devices in a mesh: section: 1, expert: 32 (over z, y, x, core).
Axes of the slice: x: 2, y: 2, z: 4, core: 2. Of those that a mesh axis runs over, the one named last changes fastest.
Arguments:
- forward_input: bfloat16 [1, 3072, 1024], P('section', 'expert'), may hold values from -6 to 6
- forward_routes: int32 [1, 3072, 6], P('section', 'expert'), may hold values from 0 to 15, all different within a row; in each aligned block of 96 rows (0 to 95, 96 to 191, ..., all dimensions but the last counted through in order) at most 42 rows name the same one
- forward_gates: float32 [1, 3072, 6], P('section', 'expert'), may hold values from 0.05 to 0.6
- backward_input: bfloat16 [1, 1536, 1024], P('section', 'expert'), may hold values from -6 to 6
- backward_routes: int32 [1, 1536, 6], P('section', 'expert'), may hold values from 0 to 15, all different within a row; in each aligned block of 48 rows (0 to 47, 48 to 95, ..., all dimensions but the last counted through in order) at most 20 rows name the same one
- backward_gates: float32 [1, 1536, 6], P('section', 'expert'), may hold values from 0.05 to 0.6
- output_grad: bfloat16 [1, 1536, 1024], P('section', 'expert'), may hold values from -6 to 6
- weight_in: bfloat16 [1, 32, 1024, 1024], P('section', 'expert'), may hold values from -0.1875 to 0.1875
- weight_down: bfloat16 [1, 32, 512, 1024], P('section', 'expert'), may hold values from -0.1875 to 0.1875
Outputs:
- forward_sent: bfloat16 [1, 3072, 1024], P('section', 'expert')
- backward_sent: bfloat16 [1, 1536, 1024], P('section', 'expert')
Inputs may be any that keep to these rules, and one draw needn't show every extreme that they name: `forward_routes`: each row names 6 different experts. Among the rows of one device (aligned blocks of 96 rows) no expert is named by more than 42 rows, and in every draw some expert is named by exactly 42 rows of some device. `backward_routes`: each row names 6 different experts. Among the rows of one device (aligned blocks of 48 rows) no expert is named by more than 20 rows, and in every draw some expert is named by exactly 20 rows of some device.
All inputs are finite; a program needn't handle non-finite values.
Results may differ from a plain program's by a relative error of at most 0.0055.
Values may be sent and summed in bfloat16 or wider, within the bound.
A program may use at most 64 MiB of HBM per device.

v0:
```python
import jax
import jax.numpy as jnp
from jax import lax
from jax.sharding import PartitionSpec as P


def passed_along(block, axis, distance):
    devices = range(lax.axis_size(axis))
    route = [((i - distance) % len(devices), i) for i in devices]
    return lax.ppermute(block, axis, route)


def half_forward(token_rows, matrix_in, matrix_down):
    hidden = jnp.dot(token_rows, matrix_in, preferred_element_type=jnp.float32)
    half_width = matrix_down.shape[0]
    active = (jax.nn.silu(hidden[:, :half_width]) * hidden[:, half_width:]).astype(jnp.bfloat16)
    return jnp.dot(active, matrix_down, preferred_element_type=jnp.float32).astype(jnp.bfloat16)


def half_backward(token_rows, cotangent, matrix_in, matrix_down):
    hidden = jnp.dot(token_rows, matrix_in, preferred_element_type=jnp.float32)
    half_width = matrix_down.shape[0]
    gate_part = hidden[:, :half_width]
    up_part = hidden[:, half_width:]
    upstream = lax.dot_general(
        cotangent, matrix_down, (((1,), (1,)), ((), ())), preferred_element_type=jnp.float32
    )
    sigmoid_gate = jax.nn.sigmoid(gate_part)
    hidden_grad = jnp.concatenate(
        [
            upstream * up_part * sigmoid_gate * (1.0 + gate_part * (1.0 - sigmoid_gate)),
            upstream * gate_part * sigmoid_gate,
        ],
        axis=1,
    ).astype(jnp.bfloat16)
    return lax.dot_general(
        hidden_grad, matrix_in, (((1,), (1,)), ((), ())), preferred_element_type=jnp.float32
    ).astype(jnp.bfloat16)


def slot_layout(routes, experts, capacity):
    flat_routes = routes.reshape(-1)
    onehot = (flat_routes[:, None] == jnp.arange(experts, dtype=jnp.int32)[None, :]).astype(
        jnp.int32
    )
    earlier = jnp.cumsum(onehot, axis=0) - onehot
    placed = jnp.sum(earlier * onehot, axis=1)
    return flat_routes * capacity + placed


def dispatch(features, slot_index, experts, capacity):
    token_count = features.shape[0]
    top_count = slot_index.shape[0] // token_count
    targets = jnp.arange(experts * capacity, dtype=jnp.int32)
    selector = (targets[:, None] == slot_index[None, :]).astype(jnp.bfloat16)
    selector = selector.reshape(experts * capacity, token_count, top_count).sum(axis=2)
    placed_rows = jnp.dot(selector, features, preferred_element_type=jnp.float32).astype(
        jnp.bfloat16
    )
    return placed_rows.reshape(experts, capacity, features.shape[1])


def combine(residual, slot_index, gate_values, expert_out):
    token_count, top_count = gate_values.shape
    model_width = expert_out.shape[-1]
    picked = expert_out.reshape(-1, model_width)[slot_index].reshape(
        token_count, top_count, model_width
    )
    mixed_out = residual.astype(jnp.float32) + jnp.sum(
        gate_values[:, :, None] * picked.astype(jnp.float32), axis=1
    )
    return mixed_out.astype(jnp.bfloat16)


def pair_sum(halves):
    return (halves[:, 0].astype(jnp.float32) + halves[:, 1].astype(jnp.float32)).astype(
        jnp.bfloat16
    )


def on_device(
    forward_input,
    forward_routes,
    forward_gates,
    backward_input,
    backward_routes,
    backward_gates,
    output_grad,
    weight_in,
    weight_down,
):
    devices = lax.axis_size("expert")
    experts = devices // 2
    matrix_in = weight_in[0, 0]
    matrix_down = weight_down[0, 0]
    ahead_tokens = forward_input[0]
    back_tokens = backward_input[0]
    back_grad = output_grad[0]
    model_width = ahead_tokens.shape[1]
    cap_ahead = 2 * (7 * ahead_tokens.shape[0] // (2 * experts))
    cap_back = 2 * (7 * back_tokens.shape[0] // (2 * experts))
    ahead_slots = slot_layout(forward_routes[0], experts, cap_ahead)
    ahead_buffer = dispatch(ahead_tokens, ahead_slots, experts, cap_ahead)
    back_slots = slot_layout(backward_routes[0], experts, cap_back)
    back_buffer = dispatch(
        jnp.concatenate([back_tokens, back_grad], axis=1), back_slots, experts, cap_back
    )
    received = lax.all_to_all(
        jnp.repeat(ahead_buffer, 2, axis=0), "expert", split_axis=0, concat_axis=0, tiled=True
    )
    item_count = received.shape[1]
    partial_value = half_forward(received.reshape(-1, model_width), matrix_in, matrix_down)
    partial_value = partial_value.reshape(devices, item_count, model_width)
    returned = lax.all_to_all(partial_value, "expert", split_axis=0, concat_axis=0, tiled=True)
    ahead_out = pair_sum(returned.reshape(experts, 2, cap_ahead, model_width))
    received = lax.all_to_all(
        jnp.repeat(back_buffer, 2, axis=0), "expert", split_axis=0, concat_axis=0, tiled=True
    )
    item_count = received.shape[1]
    flattened = received.reshape(-1, 2 * model_width)
    partial_value = half_backward(
        flattened[:, :model_width], flattened[:, model_width:], matrix_in, matrix_down
    )
    partial_value = partial_value.reshape(devices, item_count, model_width)
    returned_back = lax.all_to_all(partial_value, "expert", split_axis=0, concat_axis=0, tiled=True)
    back_out = pair_sum(returned_back.reshape(experts, 2, cap_back, model_width))
    ahead_mixed = combine(ahead_tokens, ahead_slots, forward_gates[0], ahead_out)
    back_mixed = combine(back_grad, back_slots, backward_gates[0], back_out)
    forward_sent = passed_along(ahead_mixed[None], "section", 1)
    backward_sent = passed_along(back_mixed[None], "section", -1)
    return (forward_sent, backward_sent)


def solution(mesh):
    placed = (
        P("section", "expert", None),
        P("section", "expert", None),
        P("section", "expert", None),
        P("section", "expert", None),
        P("section", "expert", None),
        P("section", "expert", None),
        P("section", "expert", None),
        P("section", "expert", None, None),
        P("section", "expert", None, None),
    )
    return jax.shard_map(
        on_device,
        mesh=mesh,
        in_specs=placed,
        out_specs=(P("section", "expert", None), P("section", "expert", None)),
        check_vma=False,
    )
```

profile of v0, /device:TPU:24, one launch (start us, length us, event | category | flops | bytes accessed | tf_op | source)
XLA Modules:
  0.0 298.0 jit_solution(4986975901760182997)
XLA Ops:
  0.6 0.0 copy-start
  0.6 0.9 copy.46
  1.6 0.1 eq.83
  1.7 0.9 reduce-window.16
  2.6 0.2 slice_reduce_fusion.1
  2.8 0.1 bitcast_bitcast_fusion.1
  3.0 0.1 reduce_sum.79
  3.1 0.1 copy.50
  3.2 0.1 fusion.26
  3.3 1.5 convolution_convert_fusion.1
  4.8 1.3 reshape.187
  6.1 3.5 %broadcast_in_dim.5 = bf16[16,2,20,2048]{3,2,1,0:T(8,128)(2,1)} broadcast(bf16[16,20,2048]{2,1,0:T(8,128)(2,1)} %reshape.187), dimensions={0,2,3} | broadcast | bytes 3932160 | tf_op jit(solution)/shard_map/broadcast_in_dim | solution.py:117
  9.5 5.9 %all-to-all-start.2 = ((bf16[32,20,2048]{2,1,0:T(8,128)(2,1)}), bf16[32,20,2048]{2,1,0:T(8,128)(2,1)}, u32[]{:S(2)}, u32[]{:S(2)}) async-start(bf16[32,20,2048]{2,1,0:T(8,128)(2,1)} %bitcast.88), calls=%async_computation.2 | async-start | bytes 6291456 | tf_op jit(solution)/shard_map/all_to_all | solution.py:116
  15.5 0.1 copy.38
  15.6 0.1 eq.73
  15.8 1.4 reduce-window.14
  17.2 0.2 slice_reduce_fusion
  17.5 0.1 bitcast_bitcast_fusion
  17.6 0.1 reduce_sum.73
  17.7 0.1 copy.42
  17.8 0.3 fusion.23
  18.1 1.5 convolution_convert_fusion.2
  19.6 1.4 reshape.180
  20.9 64.4 %all-to-all-done.2 = bf16[32,20,2048]{2,1,0:T(8,128)(2,1)} async-done(((bf16[32,20,2048]{2,1,0:T(8,128)(2,1)}), bf16[32,20,2048]{2,1,0:T(8,128)(2,1)}, u32[]{:S(2)}, u32[]{:S(2)}) %all-to-all-start.2) | async-done | bytes 2621472 | tf_op jit(solution)/shard_map/all_to_all | solution.py:116
  85.3 3.6 %broadcast_in_dim.4 = bf16[16,2,42,1024]{3,2,1,0:T(8,128)(2,1)} broadcast(bf16[16,42,1024]{2,1,0:T(8,128)(2,1)} %reshape.180), dimensions={0,2,3} | broadcast | bytes 4128768 | tf_op jit(solution)/shard_map/broadcast_in_dim | solution.py:109
  88.9 5.6 %all-to-all-start = ((bf16[32,42,1024]{2,1,0:T(8,128)(2,1)}), bf16[32,42,1024]{2,1,0:T(8,128)(2,1)}, u32[]{:S(2)}, u32[]{:S(2)}) async-start(bf16[32,42,1024]{2,1,0:T(8,128)(2,1)} %bitcast.89), calls=%async_computation | async-start | bytes 6291456 | tf_op jit(solution)/shard_map/all_to_all | solution.py:108
  94.5 5.2 %reshape.189 = bf16[640,2048]{1,0:T(8,128)(2,1)} reshape(bf16[32,20,2048]{2,1,0:T(8,128)(2,1)} %all-to-all-done.2) | data formatting | bytes 5242880 | tf_op jit(solution)/shard_map/reshape | solution.py:120
  99.8 3.4 %fusion.3 = f32[640,1024]{0,1:T(8,128)S(1)} fusion(bf16[1,1,1024,1024]{3,2,1,0:T(8,128)(2,1)S(1)} %copy-done, bf16[640,2048]{1,0:T(8,128)(2,1)} %reshape.189), kind=kOutput, calls=%fused_computation.10 | convolution fusion | flops 1342177280 | bytes 6029312 | tf_op jit(solution)/shard_map/dot_general | solution.py:21
  103.2 1.4 fusion.14
  104.5 1.6 fusion.8
  106.1 1.3 reshape.190
  107.4 57.0 %all-to-all-done = bf16[32,42,1024]{2,1,0:T(8,128)(2,1)} async-done(((bf16[32,42,1024]{2,1,0:T(8,128)(2,1)}), bf16[32,42,1024]{2,1,0:T(8,128)(2,1)}, u32[]{:S(2)}, u32[]{:S(2)}) %all-to-all-start) | async-done | bytes 2752544 | tf_op jit(solution)/shard_map/all_to_all | solution.py:108
  164.4 5.6 %all-to-all-start.3 = ((bf16[32,20,1024]{2,1,0:T(8,128)(2,1)}), bf16[32,20,1024]{2,1,0:T(8,128)(2,1)}, u32[]{:S(2)}, u32[]{:S(2)}) async-start(bf16[32,20,1024]{2,1,0:T(8,128)(2,1)} %reshape.190), calls=%async_computation.3 | async-start | bytes 3145728 | tf_op jit(solution)/shard_map/all_to_all | solution.py:125
  170.1 4.4 %reshape.182 = bf16[1344,1024]{1,0:T(8,128)(2,1)} reshape(bf16[32,42,1024]{2,1,0:T(8,128)(2,1)} %all-to-all-done) | data formatting | bytes 5505024 | tf_op jit(solution)/shard_map/reshape | solution.py:112
  174.5 4.9 %fusion.5 = f32[1344,1024]{1,0:T(8,128)S(1)} fusion(bf16[1344,1024]{1,0:T(8,128)(2,1)} %reshape.182, bf16[1,1,1024,1024]{3,2,1,0:T(8,128)(2,1)S(1)} %copy-done), kind=kOutput, calls=%fused_computation.12 | convolution fusion | flops 2818572288 | bytes 10354688 | tf_op jit(solution)/shard_map/dot_general | solution.py:14
  179.4 3.3 %convolution_convert_fusion = bf16[1344,1024]{1,0:T(8,128)(2,1)} fusion(f32[1344,1024]{1,0:T(8,128)S(1)} %fusion.5, bf16[1,1,512,1024]{3,2,1,0:T(8,128)(2,1)S(1)} %copy-done.11), kind=kOutput, calls=%fused_computation.2 | convolution fusion | flops 1414791168 | bytes 9306112 | tf_op jit(solution)/shard_map/dot_general | solution.py:17
  182.6 4.4 %reshape.183 = bf16[32,42,1024]{2,1,0:T(8,128)(2,1)} reshape(bf16[1344,1024]{1,0:T(8,128)(2,1)} %convolution_convert_fusion) | data formatting | bytes 5505024 | tf_op jit(solution)/shard_map/reshape | solution.py:113
  187.0 18.7 %all-to-all-done.3 = bf16[32,20,1024]{2,1,0:T(8,128)(2,1)} async-done(((bf16[32,20,1024]{2,1,0:T(8,128)(2,1)}), bf16[32,20,1024]{2,1,0:T(8,128)(2,1)}, u32[]{:S(2)}, u32[]{:S(2)}) %all-to-all-start.3) | async-done | bytes 1310752 | tf_op jit(solution)/shard_map/all_to_all | solution.py:125
  205.7 6.0 %all-to-all-start.1 = ((bf16[32,42,1024]{2,1,0:T(8,128)(2,1)}), bf16[32,42,1024]{2,1,0:T(8,128)(2,1)}, u32[]{:S(2)}, u32[]{:S(2)}) async-start(bf16[32,42,1024]{2,1,0:T(8,128)(2,1)} %reshape.183), calls=%async_computation.1 | async-start | bytes 6291456 | tf_op jit(solution)/shard_map/all_to_all | solution.py:114
  211.7 0.1 mul.105
  211.8 0.7 copy.56
  212.6 0.1 mul.119
  212.7 0.0 copy-done.9
  212.7 0.7 copy.57
  213.5 1.7 add_convert_fusion.1
  215.2 0.1 convert_element_type.119
  215.3 2.1 gather_fusion.1
  217.4 0.0 copy-start.6
  217.4 1.3 reshape.195
  218.7 0.0 copy-done.6
  218.7 2.6 multiply_reduce_fusion.1
  221.3 60.2 %all-to-all-done.1 = bf16[32,42,1024]{2,1,0:T(8,128)(2,1)} async-done(((bf16[32,42,1024]{2,1,0:T(8,128)(2,1)}), bf16[32,42,1024]{2,1,0:T(8,128)(2,1)}, u32[]{:S(2)}, u32[]{:S(2)}) %all-to-all-start.1) | async-done | bytes 2752544 | tf_op jit(solution)/shard_map/all_to_all | solution.py:114
  281.6 3.8 %add_convert_fusion = bf16[16,1,42,1024]{3,2,0,1:T(8,128)(2,1)} fusion(bf16[16,2,42,1024]{3,2,1,0:T(8,128)(2,1)} %bitcast.7), kind=kLoop, calls=%fused_computation.4 | loop fusion | flops 2752512 | bytes 4128768 | tf_op jit(solution)/shard_map/convert_element_type | solution.py:76
  285.3 1.6 convert_element_type.107
  286.9 3.4 %gather_fusion = bf16[576,1024]{1,0:T(8,128)(2,1)} fusion(bf16[672,1024]{1,0:T(8,128)(2,1)S(1)} %convert_element_type.107, s32[1024]{0:T(1024)S(1)} %pad_clamp_fusion.1), kind=kCustom, calls=%fused_computation | custom fusion | bytes 2361600 | tf_op jit(solution)/shard_map/gather | solution.py:66
  290.3 3.2 %reshape.193 = f32[96,6,1024]{2,1,0:T(8,128)} reshape(bf16[576,1024]{1,0:T(8,128)(2,1)} %gather_fusion) | data formatting | bytes 3538944 | tf_op jit(solution)/shard_map/convert_element_type | solution.py:70
  293.5 0.0 copy-start.4
  293.5 3.0 %multiply_reduce_fusion = f32[96,1024]{1,0:T(8,128)S(1)} fusion(f32[96,6,1024]{2,1,0:T(8,128)} %reshape.193, f32[96,6]{1,0:T(8,128)S(1)} %bitcast.91), kind=kLoop, calls=%fused_computation.3 | loop fusion | flops 1081344 | bytes 2754816 | tf_op jit(solution)/shard_map/reduce_sum | solution.py:69
  296.6 0.0 collective-permute-start
  296.7 0.0 collective-permute-start.1
  296.7 0.0 collective-permute-done.1
  296.7 0.0 collective-permute-done
  296.7 0.7 copy.72
  297.4 0.6 copy.73
  (37 shorter events, 0.3 us)
Async XLA Ops:
  0.6 99.1 %copy-start = (bf16[1,1,1024,1024]{3,2,1,0:T(8,128)(2,1)S(1)}, bf16[1,1,1024,1024]{3,2,1,0:T(8,128)(2,1)}, u32[]{:S(2)}) copy-start(bf16[1,1,1024,1024]{3,2,1,0:T(8,128)(2,1)} %param.16) | copy-start | bytes 6291460
  9.5 5.9 %copy-start.7 = (s32[1,96,6]{1,0,2:T(1,128)S(1)}, s32[1,96,6]{1,0,2:T(1,128)}, u32[]{:S(2)}) copy-start(s32[1,96,6]{1,0,2:T(1,128)} %param.10) | copy-start | bytes 6916
  9.5 75.8 %all-to-all-start.2 = ((bf16[32,20,2048]{2,1,0:T(8,128)(2,1)}), bf16[32,20,2048]{2,1,0:T(8,128)(2,1)}, u32[]{:S(2)}, u32[]{:S(2)}) async-start(bf16[32,20,2048]{2,1,0:T(8,128)(2,1)} %bitcast.88), calls=%async_computation.2 | async-start | bytes 6291456 | tf_op jit(solution)/shard_map/all_to_all | solution.py:116
  88.9 75.5 %all-to-all-start = ((bf16[32,42,1024]{2,1,0:T(8,128)(2,1)}), bf16[32,42,1024]{2,1,0:T(8,128)(2,1)}, u32[]{:S(2)}, u32[]{:S(2)}) async-start(bf16[32,42,1024]{2,1,0:T(8,128)(2,1)} %bitcast.89), calls=%async_computation | async-start | bytes 6291456 | tf_op jit(solution)/shard_map/all_to_all | solution.py:108
  99.7 3.4 %copy-start.1 = (bf16[640,2048]{1,0:T(8,128)(2,1)S(1)}, bf16[640,2048]{1,0:T(8,128)(2,1)}, u32[]{:S(2)}) copy-start(bf16[640,2048]{1,0:T(8,128)(2,1)} %reshape.189) | copy-start | bytes 7864324
  99.8 3.4 %copy-start.10 = (bf16[1,1,512,1024]{3,2,1,0:T(8,128)(2,1)S(1)}, bf16[1,1,512,1024]{3,2,1,0:T(8,128)(2,1)}, u32[]{:S(2)}) copy-start(bf16[1,1,512,1024]{3,2,1,0:T(8,128)(2,1)} %param.17) | copy-start | bytes 3145732
  164.4 41.3 %all-to-all-start.3 = ((bf16[32,20,1024]{2,1,0:T(8,128)(2,1)}), bf16[32,20,1024]{2,1,0:T(8,128)(2,1)}, u32[]{:S(2)}, u32[]{:S(2)}) async-start(bf16[32,20,1024]{2,1,0:T(8,128)(2,1)} %reshape.190), calls=%async_computation.3 | async-start | bytes 3145728 | tf_op jit(solution)/shard_map/all_to_all | solution.py:125
  174.5 4.9 %copy-start.11 = (bf16[1,1,512,1024]{3,2,1,0:T(8,128)(2,1)S(1)}, bf16[1,1,512,1024]{3,2,1,0:T(8,128)(2,1)}, u32[]{:S(2)}) copy-start(bf16[1,1,512,1024]{3,2,1,0:T(8,128)(2,1)} %param.17) | copy-start | bytes 3145732
  187.0 24.8 %copy-start.8 = (f32[1,96,6]{1,0,2:T(1,128)S(1)}, f32[1,96,6]{1,0,2:T(1,128)}, u32[]{:S(2)}) copy-start(f32[1,96,6]{1,0,2:T(1,128)} %param.11) | copy-start | bytes 6916
  187.0 25.7 %copy-start.9 = (f32[1,48,6]{1,0,2:T(1,128)S(1)}, f32[1,48,6]{1,0,2:T(1,128)}, u32[]{:S(2)}) copy-start(f32[1,48,6]{1,0,2:T(1,128)} %param.14) | copy-start | bytes 3460
  205.7 75.8 %all-to-all-start.1 = ((bf16[32,42,1024]{2,1,0:T(8,128)(2,1)}), bf16[32,42,1024]{2,1,0:T(8,128)(2,1)}, u32[]{:S(2)}, u32[]{:S(2)}) async-start(bf16[32,42,1024]{2,1,0:T(8,128)(2,1)} %reshape.183), calls=%async_computation.1 | async-start | bytes 6291456 | tf_op jit(solution)/shard_map/all_to_all | solution.py:114
  217.4 1.3 copy-start.6
  290.3 3.2 %copy-start.5 = (f32[1,96,6]{2,1,0:T(8,128)S(1)}, f32[1,96,6]{2,1,0:T(8,128)}, u32[]{:S(2)}) copy-start(f32[1,96,6]{2,1,0:T(8,128)} %copy.56) | copy-start | bytes 6916
  293.5 3.0 %copy-start.3 = (bf16[1,96,1024]{2,1,0:T(8,128)(2,1)S(1)}, bf16[1,96,1024]{2,1,0:T(8,128)(2,1)}, u32[]{:S(2)}) copy-start(bf16[1,96,1024]{2,1,0:T(8,128)(2,1)} %param.9) | copy-start | bytes 589828
  293.5 3.1 %copy-start.2 = (f32[48,1024]{1,0:T(8,128)S(1)}, f32[48,1024]{1,0:T(8,128)}, u32[]{:S(2)}) copy-start(f32[48,1024]{1,0:T(8,128)} %multiply_reduce_fusion.1) | copy-start | bytes 589828
  293.5 3.1 %copy-start.4 = (bf16[1,48,1024]{2,1,0:T(8,128)(2,1)S(1)}, bf16[1,48,1024]{2,1,0:T(8,128)(2,1)}, u32[]{:S(2)}) copy-start(bf16[1,48,1024]{2,1,0:T(8,128)(2,1)} %param.15) | copy-start | bytes 294916
  296.6 0.1 collective-permute-start
  (1 other events, 0.0 us)
where the time goes:
time: 302 us; the launch traced here: 298 us
  waiting for transfers between devices  200 us (66%)
  local copies, waits for them, and re-layouts  41.9 us (14%)
  starting transfers between devices  23.2 us (8%)
  matrix products  17.4 us (6%)
  other arithmetic  14.3 us (5%)
    all_to_all x2, waiting for transfers between devices, on_device(): lax.all_to_all(partial_value, 'expert', split_axis=0, concat_axis=0, tile...  78.9 us
    all_to_all x1, waiting for transfers between devices, on_device(): lax.all_to_all(jnp.repeat(back_buffer, 2, axis=0), 'expert', split_axis=0...  64.4 us
    all_to_all x1, waiting for transfers between devices, on_device(): lax.all_to_all(jnp.repeat(ahead_buffer, 2, axis=0), 'expert', split_axis=...  57 us
    all_to_all x2, starting transfers between devices, on_device(): lax.all_to_all(partial_value, 'expert', split_axis=0, concat_axis=0, tile...  11.6 us
  transfers between devices with their start and end apart: 6, of which 4 were waited for; matrix products, arithmetic and copies ran while one was open for 15% of the time, Pallas kernels for 0%

commit v1 on v0

v1 whole, which is shorter than its diff:
```python
import functools
import jax
import jax.numpy as jnp
from jax import lax
from jax.experimental import pallas as pl
from jax.experimental.pallas import tpu as pltpu
from jax.sharding import PartitionSpec as P

PLANE = 4
NONE = -512.0
BF = jnp.bfloat16
F32 = jnp.float32
MESH = pl.DeviceIdType.MESH


def up16(count):
    return -(-count // 16) * 16


def dot(a, b):
    return jnp.dot(a, b, preferred_element_type=F32)


def dot_t(a, b):
    return lax.dot_general(a, b, (((1,), (1,)), ((), ())), preferred_element_type=F32)


def t_dot(a, b):
    return lax.dot_general(a, b, (((0,), (0,)), ((), ())), preferred_element_type=F32)


def iota(shape, dim):
    return lax.broadcasted_iota(jnp.int32, shape, dim)


def kernel(
    depth, experts, cap_f, cap_b,
    routes, gates, tok_f, tok_b, grad_b, w_in, w_down,
    out_f, out_b,
    blocks, send_d, recv_d, send_r, recv_r, send_p, recv_p, mine, acc_f, acc_b, own_f, own_b, wi, wd,
    sem_load, sem_ws, sem_wr, sem_gs, sem_gr, sem_ds, sem_dr, sem_rs, sem_rr, sem_ps, sem_pr,
):
    nf, width = tok_f.shape
    nb = tok_b.shape[0]
    half = w_down.shape[0]
    rf = up16(cap_f)
    rp = up16(2 * cap_b)
    rb = up16(cap_b)
    sec = lax.axis_index("section")
    me = lax.axis_index("expert")
    c = me % 2
    p = (me // 2) % PLANE
    z = me // (2 * PLANE)

    def dev(zz, pp, cc):
        return (sec, (zz * PLANE + pp) * 2 + cc)

    row_b, row_g, row_f = experts, experts + nb, experts + 2 * nb
    loads = [
        pltpu.make_async_copy(tok_b, blocks.at[z, pl.ds(row_b, nb)], sem_load.at[0]),
        pltpu.make_async_copy(grad_b, blocks.at[z, pl.ds(row_g, nb)], sem_load.at[1]),
        pltpu.make_async_copy(tok_f, blocks.at[z, pl.ds(row_f, nf)], sem_load.at[2]),
        pltpu.make_async_copy(w_in, wi.at[c], sem_load.at[3]),
        pltpu.make_async_copy(w_down, wd.at[c], sem_load.at[4]),
    ]
    for load in loads:
        load.start()

    barrier = pltpu.get_barrier_semaphore()
    pl.semaphore_signal(barrier, inc=1, device_id=dev(z, p, 1 - c), device_id_type=MESH)
    for q in range(1, PLANE):
        pl.semaphore_signal(
            barrier, inc=1, device_id=dev(z, (p + q) % PLANE, c), device_id_type=MESH
        )
    for q in range(1, depth):
        pl.semaphore_signal(
            barrier, inc=1, device_id=dev((z + q) % depth, p, c), device_id_type=MESH
        )

    lanes = routes.shape[1]
    e_ids = iota((experts, lanes), 0)
    named = jnp.zeros((experts, lanes), F32)
    weight = jnp.zeros((experts, lanes), F32)
    for k in range(routes.shape[0]):
        hit = routes[k : k + 1, :] == e_ids
        named = named + jnp.where(hit, 1.0, 0.0)
        weight = weight + jnp.where(hit, gates[k : k + 1, :], 0.0)
    first, second = iota((lanes, lanes), 0), iota((lanes, lanes), 1)
    earlier = jnp.where((first < second) & (first // 128 == second // 128), 1.0, 0.0).astype(BF)
    rank = dot(named.astype(BF), earlier)
    high = weight.astype(BF)
    low = (weight - high.astype(F32)).astype(BF)
    code = jnp.where(named > 0.0, rank, NONE).astype(BF)
    blocks[z, 0:experts, :] = jnp.concatenate(
        [code, high, low, jnp.zeros((experts, width - 3 * lanes), BF)], axis=1
    )

    pl.semaphore_wait(barrier, 1 + (PLANE - 1) + (depth - 1))

    weight_copies = [
        pltpu.make_async_remote_copy(
            w_in, wi.at[c], sem_ws.at[0], sem_wr.at[0], device_id=dev(z, p, 1 - c), device_id_type=MESH
        ),
        pltpu.make_async_remote_copy(
            w_down, wd.at[c], sem_ws.at[1], sem_wr.at[1], device_id=dev(z, p, 1 - c), device_id_type=MESH
        ),
    ]
    for load in loads[:3]:
        load.wait()

    def source(k):
        near = jnp.minimum(z, depth - 1 - z)
        side = jnp.where(k % 2 == 1, z - (k + 1) // 2, z + k // 2)
        far = jnp.where(2 * z < depth, k, depth - 1 - k)
        return jnp.where(k <= 2 * near, side, far)

    def relay(zs, way):
        return pltpu.make_async_remote_copy(
            blocks.at[zs], blocks.at[zs], sem_gs.at[zs, way], sem_gr.at[zs],
            device_id=dev((z + 1 if way else z + depth - 1) % depth, p, c), device_id_type=MESH,
        )

    def goes_right(zs):
        return (zs <= z) & (z < depth - 1)

    def goes_left(zs):
        return (zs >= z) & (z > 0)

    def send_on(zs):
        @pl.when(goes_right(zs))
        def _():
            relay(zs, 1).start()

        @pl.when(goes_left(zs))
        def _():
            relay(zs, 0).start()

    def dispatch_copy(zs, q):
        tgt = (p + q) % PLANE
        return pltpu.make_async_remote_copy(
            send_d.at[zs, tgt], recv_d.at[zs, p], sem_ds.at[zs, q], sem_dr.at[zs, p],
            device_id=dev(z, tgt, c), device_id_type=MESH,
        )

    def dispatch_arrival(zs, q):
        other = (p + q) % PLANE
        return pltpu.make_async_remote_copy(
            send_d.at[zs, other], recv_d.at[zs, other], sem_ds.at[zs, q], sem_dr.at[zs, other],
            device_id=dev(z, other, c), device_id_type=MESH,
        )

    def return_copy(zs, q):
        tgt = (p + q) % PLANE
        return pltpu.make_async_remote_copy(
            send_r.at[zs, tgt], recv_r.at[zs, p], sem_rs.at[zs, q], sem_rr.at[zs, p],
            device_id=dev(z, tgt, c), device_id_type=MESH,
        )

    def return_arrival(zs, q):
        other = (p + q) % PLANE
        return pltpu.make_async_remote_copy(
            send_r.at[zs, other], recv_r.at[zs, other], sem_rs.at[zs, q], sem_rr.at[zs, other],
            device_id=dev(z, other, c), device_id_type=MESH,
        )

    def part_copy(zs):
        return pltpu.make_async_remote_copy(
            send_p.at[zs], recv_p.at[z], sem_ps.at[zs], sem_pr.at[z],
            device_id=dev(zs, p, c), device_id_type=MESH,
        )

    def part_arrival(zs):
        return pltpu.make_async_remote_copy(
            send_p.at[zs], recv_p.at[zs], sem_ps.at[zs], sem_pr.at[zs],
            device_id=dev(zs, p, c), device_id_type=MESH,
        )

    def spread(zs, rows):
        total = PLANE * rows
        pick = jnp.where(
            iota((total, experts), 1) == z * PLANE + iota((total, experts), 0) // rows, 1.0, 0.0
        ).astype(BF)
        return dot(pick, blocks[zs, 0:experts, 0 : 3 * lanes])

    def slot(total, rows, count):
        return (iota((total, count), 0) % rows).astype(F32)

    def select(zs):
        table_f = spread(zs, rf)[:, 0:nf]
        pick_f = jnp.where(table_f == slot(PLANE * rf, rf, nf), 1.0, 0.0).astype(BF)
        rows_f = dot(pick_f, blocks[zs, row_f : row_f + nf, :]).astype(BF)
        table_b = spread(zs, rp)[:, 128 : 128 + nb]
        place = slot(PLANE * rp, rp, nb)
        pick_x = jnp.where(table_b == place, 1.0, 0.0).astype(BF)
        pick_g = jnp.where(table_b + cap_b == place, 1.0, 0.0).astype(BF)
        rows_b = (
            dot(pick_x, blocks[zs, row_b : row_b + nb, :])
            + dot(pick_g, blocks[zs, row_g : row_g + nb, :])
        ).astype(BF)
        for q in range(PLANE):
            send_d[zs, q, 0:rf, :] = rows_f[q * rf : (q + 1) * rf]
            send_d[zs, q, rf : rf + rp, :] = rows_b[q * rp : (q + 1) * rp]
        for q in range(1, PLANE):
            dispatch_copy(zs, q).start()
        recv_d[zs, p] = send_d[zs, p]

    def expert(zs):
        for q in range(1, PLANE):
            dispatch_arrival(zs, q).wait_recv()
        got = recv_d[zs]
        rows_f = got[:, 0:rf, :].reshape(PLANE * rf, width)
        rows_b = got[:, rf : rf + rp, :].reshape(PLANE * rp, width)
        shape = (PLANE * rb, PLANE * rp)
        row, col = iota(shape, 0), iota(shape, 1)
        same = (row // rb == col // rp) & (row % rb < cap_b)
        rows_x = dot(jnp.where(same & (col % rp == row % rb), 1.0, 0.0).astype(BF), rows_b)
        rows_g = dot(jnp.where(same & (col % rp == row % rb + cap_b), 1.0, 0.0).astype(BF), rows_b)
        mf, mb = PLANE * rf, PLANE * rb
        mine[0:mf] = rows_f
        mine[mf : mf + mb] = rows_x.astype(BF)
        mine[mf + mb : mf + 2 * mb] = rows_g.astype(BF)

        def one_half(h, carry):
            hidden = dot(mine[0 : mf + mb], wi[h])
            a, b = hidden[:, :half], hidden[:, half:]
            q = jax.nn.sigmoid(a)
            active = (a[:mf] * q[:mf] * b[:mf]).astype(BF)
            part_f = dot(active, wd[h])
            u = dot_t(mine[mf + mb : mf + 2 * mb], wd[h])
            a, b, q = a[mf:], b[mf:], q[mf:]
            grad = jnp.concatenate([u * b * q * (1.0 + a * (1.0 - q)), u * a * q], axis=1)
            part_b = dot_t(grad.astype(BF), wi[h])

            @pl.when(h == 0)
            def _():
                acc_f[...] = part_f
                acc_b[...] = part_b

            @pl.when(h == 1)
            def _():
                total_f = (acc_f[...] + part_f).astype(BF)
                total_b = (acc_b[...] + part_b).astype(BF)
                for j in range(PLANE):
                    send_r[zs, j, 0:rf, :] = total_f[j * rf : (j + 1) * rf]
                    send_r[zs, j, rf : rf + rb, :] = total_b[j * rb : (j + 1) * rb]

            return carry

        lax.fori_loop(0, 2, one_half, 0)
        for q in range(1, PLANE):
            return_copy(zs, q).start()
        recv_r[zs, p] = send_r[zs, p]

    def weigh(table, place, rows, count, lane):
        hit = table[:, lane : lane + count] == place
        high_part = jnp.where(hit, table[:, lanes + lane : lanes + lane + count], 0.0)
        low_part = jnp.where(hit, table[:, 2 * lanes + lane : 2 * lanes + lane + count], 0.0)
        return t_dot(high_part.astype(BF), rows) + t_dot(low_part.astype(BF), rows)

    def combine(zs):
        for q in range(1, PLANE):
            return_arrival(zs, q).wait_recv()
        got = recv_r[zs]
        rows_f = got[:, 0:rf, :].reshape(PLANE * rf, width)
        rows_b = got[:, rf : rf + rb, :].reshape(PLANE * rb, width)
        part_f = weigh(spread(zs, rf), slot(PLANE * rf, rf, nf), rows_f, nf, 0)
        part_b = weigh(spread(zs, rb), slot(PLANE * rb, rb, nb), rows_b, nb, 128)

        @pl.when(zs == z)
        def _():
            own_f[...] = part_f
            own_b[...] = part_b

        @pl.when(zs != z)
        def _():
            send_p[zs, 0:nf, :] = part_f.astype(BF)
            send_p[zs, nf : nf + nb, :] = part_b.astype(BF)
            part_copy(zs).start()

    def step(k, carry):
        @pl.when(k < depth)
        def _():
            zs = source(k)

            @pl.when(zs != z)
            def _():
                relay(zs, 0).wait_recv()

            send_on(zs)

            @pl.when(k == 0)
            def _():
                for copy in weight_copies:
                    copy.start()

            select(zs)

        @pl.when((k >= 1) & (k <= depth))
        def _():
            @pl.when(k == 1)
            def _():
                for load in loads[3:]:
                    load.wait()
                for copy in weight_copies:
                    copy.wait_recv()

            expert(source(k - 1))

        @pl.when(k >= 2)
        def _():
            combine(source(k - 2))

        return carry

    lax.fori_loop(0, depth + 2, step, 0)

    total_f = blocks[z, row_f : row_f + nf, :].astype(F32)
    total_b = blocks[z, row_g : row_g + nb, :].astype(F32)
    for q in range(1, depth):
        zs = (z + q) % depth
        part_arrival(zs).wait_recv()
        total_f = total_f + recv_p[zs, 0:nf, :].astype(F32)
        total_b = total_b + recv_p[zs, nf : nf + nb, :].astype(F32)
    out_f[...] = (total_f + own_f[...]).astype(BF)
    out_b[...] = (total_b + own_b[...]).astype(BF)

    for copy in weight_copies:
        copy.wait_send()

    def drain(zs, carry):
        @pl.when(goes_right(zs))
        def _():
            relay(zs, 1).wait_send()

        @pl.when(goes_left(zs))
        def _():
            relay(zs, 0).wait_send()

        for q in range(1, PLANE):
            dispatch_copy(zs, q).wait_send()
            return_copy(zs, q).wait_send()

        @pl.when(zs != z)
        def _():
            part_copy(zs).wait_send()

        return carry

    lax.fori_loop(0, depth, drain, 0)


def passed_along(block, axis, distance):
    count = lax.axis_size(axis)
    if count == 1:
        return block
    route = [((i - distance) % count, i) for i in range(count)]
    return lax.ppermute(block, axis, route)


def side_by_side(ahead, back, fill):
    def padded(array):
        return jnp.pad(array.T, ((0, 0), (0, 128 - array.shape[0])), constant_values=fill)

    return jnp.concatenate([padded(ahead), padded(back)], axis=1)


def on_device(
    forward_input, forward_routes, forward_gates,
    backward_input, backward_routes, backward_gates,
    output_grad, weight_in, weight_down,
):
    devices = lax.axis_size("expert")
    experts = devices // 2
    depth = experts // PLANE
    nf, width = forward_input.shape[1:]
    nb = backward_input.shape[1]
    half = weight_down.shape[2]
    cap_f = 2 * (7 * nf // (2 * experts))
    cap_b = 2 * (7 * nb // (2 * experts))
    rf, rp, rb = up16(cap_f), up16(2 * cap_b), up16(cap_b)
    routes = side_by_side(forward_routes[0], backward_routes[0], -1)
    gates = side_by_side(forward_gates[0], backward_gates[0], 0.0)
    vmem = pl.BlockSpec(memory_space=pltpu.VMEM)
    anywhere = pl.BlockSpec(memory_space=pl.ANY)
    dma = pltpu.SemaphoreType.DMA
    ahead, back = pl.pallas_call(
        functools.partial(kernel, depth, experts, cap_f, cap_b),
        out_shape=(
            jax.ShapeDtypeStruct((nf, width), BF),
            jax.ShapeDtypeStruct((nb, width), BF),
        ),
        in_specs=[vmem] * 2 + [anywhere] * 5,
        out_specs=(vmem, vmem),
        scratch_shapes=[
            pltpu.VMEM((depth, experts + 2 * nb + nf, width), BF),
            pltpu.VMEM((depth, PLANE, rf + rp, width), BF),
            pltpu.VMEM((depth, PLANE, rf + rp, width), BF),
            pltpu.VMEM((depth, PLANE, rf + rb, width), BF),
            pltpu.VMEM((depth, PLANE, rf + rb, width), BF),
            pltpu.VMEM((depth, nf + nb, width), BF),
            pltpu.VMEM((depth, nf + nb, width), BF),
            pltpu.VMEM((PLANE * (rf + 2 * rb), width), BF),
            pltpu.VMEM((PLANE * rf, width), F32),
            pltpu.VMEM((PLANE * rb, width), F32),
            pltpu.VMEM((nf, width), F32),
            pltpu.VMEM((nb, width), F32),
            pltpu.VMEM((2, width, 2 * half), BF),
            pltpu.VMEM((2, half, width), BF),
            dma((5,)),
            dma((2,)),
            dma((2,)),
            dma((depth, 2)),
            dma((depth,)),
            dma((depth, PLANE)),
            dma((depth, PLANE)),
            dma((depth, PLANE)),
            dma((depth, PLANE)),
            dma((depth,)),
            dma((depth,)),
        ],
        compiler_params=pltpu.CompilerParams(
            collective_id=0, has_side_effects=True, vmem_limit_bytes=56 * 1024 * 1024
        ),
    )(
        routes, gates, forward_input[0], backward_input[0], output_grad[0],
        weight_in[0, 0], weight_down[0, 0],
    )
    forward_sent = passed_along(ahead[None], "section", 1)
    backward_sent = passed_along(back[None], "section", -1)
    return (forward_sent, backward_sent)


def solution(mesh):
    rows = P("section", "expert", None)
    weights = P("section", "expert", None, None)
    return jax.shard_map(
        on_device,
        mesh=mesh,
        in_specs=(rows,) * 7 + (weights,) * 2,
        out_specs=(rows, rows),
        check_vma=False,
    )
```

time: 302 us -> 97.9 us (0.32); the launches traced: 298 us -> 97.6 us
  waiting for transfers between devices: 200 us -> 0 us
  Pallas kernels: 0 us -> 89.8 us
  local copies, waits for them, and re-layouts: 41.9 us -> 5.9 us
  starting transfers between devices: 23.2 us -> 0 us
  matrix products: 17.4 us -> 0 us
  other arithmetic: 14.3 us -> 1.21 us
    all_to_all x4 -> x0, waiting for transfers between devices: 200 us -> none  [the longest x2 78.9 us: on_device(): lax.all_to_all(partial_value, 'expert', split_axis=0, concat_axis=0, tile...]
    pallas_call x0 -> x1, Pallas kernels: none -> 89.8 us  [on_device(): pl.pallas_call(functools.partial(kernel, depth, experts, cap_f, cap_b), o...]
    all_to_all x4 -> x0, starting transfers between devices: 23.1 us -> none  [the longest x2 11.6 us: on_device(): lax.all_to_all(partial_value, 'expert', split_axis=0, concat_axis=0, tile...]
    reshape x6 -> x0, local copies, waits for them, and re-layouts: 18 us -> none  [the longest x2 5.71 us: on_device(): partial_value = partial_value.reshape(devices, item_count, model_width)]
    dot_general x7 -> x0, matrix products: 17.4 us -> none  [the longest x1 4.88 us: half_forward(): hidden = jnp.dot(token_rows, matrix_in, preferred_element_type=jnp.float32)]
    broadcast_in_dim x2 -> x0, local copies, waits for them, and re-layouts: 7.05 us -> none  [the longest x1 3.57 us: on_device(): jnp.repeat(ahead_buffer, 2, axis=0)]
    convert_element_type x4 -> x0, local copies, waits for them, and re-layouts: 6.21 us -> none  [the longest x2 4.5 us: combine(): picked.astype(jnp.float32)]
    reduce_sum x6 -> x0, other arithmetic: 6.13 us -> none  [the longest x2 5.66 us: combine(): jnp.sum(gate_values[:, :, None] * picked.astype(jnp.float32), axis=1)]
  transfers between devices with their start and end apart: 6 -> 0, of which waited for: 4 -> 0; matrix products, arithmetic and copies ran while one was open for 15% -> 0% of each run, Pallas kernels for 0% -> 0%
where the time goes in v1:
time: 97.9 us; the launch traced here: 97.6 us
  Pallas kernels  89.8 us (92%)
  local copies, waits for them, and re-layouts  5.9 us (6%)
  other arithmetic  1.21 us (1%)
    pallas_call x1, Pallas kernels, on_device(): pl.pallas_call(functools.partial(kernel, depth, experts, cap_f, cap_b), o...  89.8 us
    unnamed x6, local copies, waits for them, and re-layouts  5.9 us

profile of v1, /device:TPU:24, one launch (start us, length us, event | category | flops | bytes accessed | tf_op | source)
XLA Modules:
  0.0 97.6 jit_solution(673964545292615126)
XLA Ops:
  0.6 0.7 copy.22
  1.3 0.7 copy.20
  2.0 0.7 copy.21
  2.7 0.6 select_add_fusion.routes
  3.3 0.7 copy.19
  4.0 0.6 select_maximum_fusion.gates
  4.6 89.8 %shard_map.104 = (bf16[96,1024]{1,0:T(8,128)(2,1)}, bf16[48,1024]{1,0:T(8,128)(2,1)}) custom-call(s32[6,256]{1,0:T(8,128)} %select_add_fusion.routes, f32[6,256]{1,0:T(8,128)} %select_maximum_fusion.gates, bf16[96,1024]{1,0:T(8,128)(2,1)} %bitcast.29, bf16[48,1024]{1,0:T(8,128)(2,1)} %bitcast.31, bf16[48,1024]{1,0:T(8,128)(2,1)} %bitcast.32, ...), custom_call_target="tpu_custom_call" | custom-call | tf_op jit(solution)/shard_map/pallas_call | solution.py:386
  94.4 1.6 %copy.25 = bf16[1,96,1024]{2,1,0:T(8,128)(2,1)} copy(bf16[1,96,1024]{2,1,0:T(8,128)(2,1)} %bitcast.30) | data formatting | bytes 393216
  96.0 1.5 %copy.26 = bf16[1,48,1024]{2,1,0:T(8,128)(2,1)} copy(bf16[1,48,1024]{2,1,0:T(8,128)(2,1)} %bitcast.33) | data formatting | bytes 196608

commit v2 on v1

--- a/solution.py
+++ b/solution.py
@@ -35,7 +35,7 @@
 
 def kernel(
     depth, experts, cap_f, cap_b,
-    routes, gates, tok_f, tok_b, grad_b, w_in, w_down,
+    routes_f, gates_f, routes_b, gates_b, tok_f, tok_b, grad_b, w_in, w_down,
     out_f, out_b,
     blocks, send_d, recv_d, send_r, recv_r, send_p, recv_p, mine, acc_f, acc_b, own_f, own_b, wi, wd,
     sem_load, sem_ws, sem_wr, sem_gs, sem_gr, sem_ds, sem_dr, sem_rs, sem_rr, sem_ps, sem_pr,
@@ -46,6 +46,7 @@
     rf = up16(cap_f)
     rp = up16(2 * cap_b)
     rb = up16(cap_b)
+    rr = up16(cap_f + cap_b)
     sec = lax.axis_index("section")
     me = lax.axis_index("expert")
     c = me % 2
@@ -77,23 +78,25 @@
             barrier, inc=1, device_id=dev((z + q) % depth, p, c), device_id_type=MESH
         )
 
-    lanes = routes.shape[1]
-    e_ids = iota((experts, lanes), 0)
-    named = jnp.zeros((experts, lanes), F32)
-    weight = jnp.zeros((experts, lanes), F32)
-    for k in range(routes.shape[0]):
-        hit = routes[k : k + 1, :] == e_ids
-        named = named + jnp.where(hit, 1.0, 0.0)
-        weight = weight + jnp.where(hit, gates[k : k + 1, :], 0.0)
-    first, second = iota((lanes, lanes), 0), iota((lanes, lanes), 1)
-    earlier = jnp.where((first < second) & (first // 128 == second // 128), 1.0, 0.0).astype(BF)
-    rank = dot(named.astype(BF), earlier)
-    high = weight.astype(BF)
-    low = (weight - high.astype(F32)).astype(BF)
-    code = jnp.where(named > 0.0, rank, NONE).astype(BF)
-    blocks[z, 0:experts, :] = jnp.concatenate(
-        [code, high, low, jnp.zeros((experts, width - 3 * lanes), BF)], axis=1
-    )
+    lanes = 256
+    blocks[z, 0:experts, :] = jnp.zeros((experts, width), BF)
+    for routes, gates, lane in ((routes_f, gates_f, 0), (routes_b, gates_b, 128)):
+        count = routes.shape[2]
+        e_ids = iota((experts, count), 0)
+        named = jnp.zeros((experts, count), F32)
+        weight = jnp.zeros((experts, count), F32)
+        for k in range(routes.shape[0]):
+            hit = routes[k] == e_ids
+            named = named + jnp.where(hit, 1.0, 0.0)
+            weight = weight + jnp.where(hit, gates[k], 0.0)
+        earlier = jnp.where(iota((count, count), 0) < iota((count, count), 1), 1.0, 0.0)
+        rank = dot(named.astype(BF), earlier.astype(BF))
+        high = weight.astype(BF)
+        low = (weight - high.astype(F32)).astype(BF)
+        code = jnp.where(named > 0.0, rank, NONE).astype(BF)
+        for part, values in enumerate((code, high, low)):
+            start = part * lanes + lane
+            blocks[z, 0:experts, start : start + count] = values
 
     pl.semaphore_wait(barrier, 1 + (PLANE - 1) + (depth - 1))
 
@@ -204,6 +207,12 @@
             dispatch_copy(zs, q).start()
         recv_d[zs, p] = send_d[zs, p]
 
+    def pack(rows, start, count):
+        row, col = iota((PLANE * rr, PLANE * rows), 0), iota((PLANE * rr, PLANE * rows), 1)
+        place = row % rr - start
+        hit = (row // rr == col // rows) & (place == col % rows) & (place >= 0) & (place < count)
+        return jnp.where(hit, 1.0, 0.0).astype(BF)
+
     def expert(zs):
         for q in range(1, PLANE):
             dispatch_arrival(zs, q).wait_recv()
@@ -240,9 +249,10 @@
             def _():
                 total_f = (acc_f[...] + part_f).astype(BF)
                 total_b = (acc_b[...] + part_b).astype(BF)
+                packed = dot(pack(rf, 0, cap_f), total_f) + dot(pack(rb, cap_f, cap_b), total_b)
+                packed = packed.astype(BF)
                 for j in range(PLANE):
-                    send_r[zs, j, 0:rf, :] = total_f[j * rf : (j + 1) * rf]
-                    send_r[zs, j, rf : rf + rb, :] = total_b[j * rb : (j + 1) * rb]
+                    send_r[zs, j] = packed[j * rr : (j + 1) * rr]
 
             return carry
 
@@ -260,11 +270,10 @@
     def combine(zs):
         for q in range(1, PLANE):
             return_arrival(zs, q).wait_recv()
-        got = recv_r[zs]
-        rows_f = got[:, 0:rf, :].reshape(PLANE * rf, width)
-        rows_b = got[:, rf : rf + rb, :].reshape(PLANE * rb, width)
-        part_f = weigh(spread(zs, rf), slot(PLANE * rf, rf, nf), rows_f, nf, 0)
-        part_b = weigh(spread(zs, rb), slot(PLANE * rb, rb, nb), rows_b, nb, 128)
+        rows = recv_r[zs].reshape(PLANE * rr, width)
+        table = spread(zs, rr)
+        part_f = weigh(table, slot(PLANE * rr, rr, nf), rows, nf, 0)
+        part_b = weigh(table, slot(PLANE * rr, rr, nb) - cap_f, rows, nb, 128)
 
         @pl.when(zs == z)
         def _():
@@ -295,24 +304,24 @@
 
             select(zs)
 
-        @pl.when((k >= 1) & (k <= depth))
-        def _():
-            @pl.when(k == 1)
+        @pl.when((k >= 2) & (k <= depth + 1))
+        def _():
+            @pl.when(k == 2)
             def _():
                 for load in loads[3:]:
                     load.wait()
                 for copy in weight_copies:
                     copy.wait_recv()
 
-            expert(source(k - 1))
-
-        @pl.when(k >= 2)
-        def _():
-            combine(source(k - 2))
+            expert(source((k - 1) % depth))
+
+        @pl.when(k >= 3)
+        def _():
+            combine(source((k - 2) % depth))
 
         return carry
 
-    lax.fori_loop(0, depth + 2, step, 0)
+    lax.fori_loop(0, depth + 3, step, 0)
 
     total_f = blocks[z, row_f : row_f + nf, :].astype(F32)
     total_b = blocks[z, row_g : row_g + nb, :].astype(F32)
@@ -355,13 +364,6 @@
         return block
     route = [((i - distance) % count, i) for i in range(count)]
     return lax.ppermute(block, axis, route)
-
-
-def side_by_side(ahead, back, fill):
-    def padded(array):
-        return jnp.pad(array.T, ((0, 0), (0, 128 - array.shape[0])), constant_values=fill)
-
-    return jnp.concatenate([padded(ahead), padded(back)], axis=1)
 
 
 def on_device(
@@ -378,8 +380,11 @@
     cap_f = 2 * (7 * nf // (2 * experts))
     cap_b = 2 * (7 * nb // (2 * experts))
     rf, rp, rb = up16(cap_f), up16(2 * cap_b), up16(cap_b)
-    routes = side_by_side(forward_routes[0], backward_routes[0], -1)
-    gates = side_by_side(forward_gates[0], backward_gates[0], 0.0)
+    rr = up16(cap_f + cap_b)
+    tables = [
+        jnp.transpose(array, (2, 0, 1))
+        for array in (forward_routes, forward_gates, backward_routes, backward_gates)
+    ]
     vmem = pl.BlockSpec(memory_space=pltpu.VMEM)
     anywhere = pl.BlockSpec(memory_space=pl.ANY)
     dma = pltpu.SemaphoreType.DMA
@@ -389,14 +394,14 @@
             jax.ShapeDtypeStruct((nf, width), BF),
             jax.ShapeDtypeStruct((nb, width), BF),
         ),
-        in_specs=[vmem] * 2 + [anywhere] * 5,
+        in_specs=[vmem] * 4 + [anywhere] * 5,
         out_specs=(vmem, vmem),
         scratch_shapes=[
             pltpu.VMEM((depth, experts + 2 * nb + nf, width), BF),
             pltpu.VMEM((depth, PLANE, rf + rp, width), BF),
             pltpu.VMEM((depth, PLANE, rf + rp, width), BF),
-            pltpu.VMEM((depth, PLANE, rf + rb, width), BF),
-            pltpu.VMEM((depth, PLANE, rf + rb, width), BF),
+            pltpu.VMEM((depth, PLANE, rr, width), BF),
+            pltpu.VMEM((depth, PLANE, rr, width), BF),
             pltpu.VMEM((depth, nf + nb, width), BF),
             pltpu.VMEM((depth, nf + nb, width), BF),
             pltpu.VMEM((PLANE * (rf + 2 * rb), width), BF),
@@ -422,7 +427,7 @@
             collective_id=0, has_side_effects=True, vmem_limit_bytes=56 * 1024 * 1024
         ),
     )(
-        routes, gates, forward_input[0], backward_input[0], output_grad[0],
+        *tables, forward_input[0], backward_input[0], output_grad[0],
         weight_in[0, 0], weight_down[0, 0],
     )
     forward_sent = passed_along(ahead[None], "section", 1)

time: 97.9 us -> 84.3 us (0.86)
  Pallas kernels: 89.8 us -> 80.3 us
  local copies, waits for them, and re-layouts: 5.9 us -> 3.16 us
  other arithmetic: 1.21 us -> 0 us
    pallas_call x1, Pallas kernels: 89.8 us -> 80.3 us  [on_device(): pl.pallas_call(functools.partial(kernel, depth, experts, cap_f, cap_b), o...]
    unnamed x6 -> x2, local copies, waits for them, and re-layouts: 5.9 us -> 3.16 us
    concatenate x2 -> x0, other arithmetic: 1.21 us -> none  [side_by_side(): return jnp.concatenate([padded(ahead), padded(back)], axis=1)]
where the time goes in v2:
time: 84.3 us; the launch traced here: 84.1 us
  Pallas kernels  80.3 us (95%)
  local copies, waits for them, and re-layouts  3.16 us (4%)
    pallas_call x1, Pallas kernels, on_device(): pl.pallas_call(functools.partial(kernel, depth, experts, cap_f, cap_b), o...  80.3 us
    unnamed x2, local copies, waits for them, and re-layouts  3.16 us

profile of v2, /device:TPU:24, one launch (start us, length us, event | category | flops | bytes accessed | tf_op | source)
XLA Modules:
  0.0 84.1 jit_solution(16395026644932438603)
XLA Ops:
  0.6 80.3 %shard_map.104 = (bf16[96,1024]{1,0:T(8,128)(2,1)}, bf16[48,1024]{1,0:T(8,128)(2,1)}) custom-call(s32[6,1,96]{2,1,0:T(1,128)} %bitcast.18, f32[6,1,96]{2,1,0:T(1,128)} %bitcast.19, s32[6,1,48]{2,1,0:T(1,128)} %bitcast.20, f32[6,1,48]{2,1,0:T(1,128)} %bitcast.21, bf16[96,1024]{1,0:T(8,128)(2,1)} %bitcast.14, bf16[48,1024]{1,0:T(8,128)(2,1)} %bitcast.15, ...), custom_call_target="tpu_custom_call" | custom-call | tf_op jit(solution)/shard_map/pallas_call | solution.py:391
  80.9 1.6 %copy.13 = bf16[1,96,1024]{2,1,0:T(8,128)(2,1)} copy(bf16[1,96,1024]{2,1,0:T(8,128)(2,1)} %bitcast.13) | data formatting | bytes 393216
  82.6 1.5 %copy.14 = bf16[1,48,1024]{2,1,0:T(8,128)(2,1)} copy(bf16[1,48,1024]{2,1,0:T(8,128)(2,1)} %bitcast.17) | data formatting | bytes 196608

commit v3 on v2

--- a/solution.py
+++ b/solution.py
@@ -129,6 +129,9 @@
     def goes_left(zs):
         return (zs >= z) & (z > 0)
 
+    def passes_through(zs):
+        return (zs != z) & (goes_right(zs) | goes_left(zs))
+
     def send_on(zs):
         @pl.when(goes_right(zs))
         def _():
@@ -291,18 +294,26 @@
         def _():
             zs = source(k)
 
-            @pl.when(zs != z)
+            @pl.when((zs != z) & jnp.logical_not(passes_through(zs)))
             def _():
                 relay(zs, 0).wait_recv()
 
-            send_on(zs)
-
             @pl.when(k == 0)
             def _():
+                send_on(zs)
                 for copy in weight_copies:
                     copy.start()
 
             select(zs)
+
+        @pl.when(k < depth - 1)
+        def _():
+            after = source(k + 1)
+
+            @pl.when(passes_through(after))
+            def _():
+                relay(after, 0).wait_recv()
+                send_on(after)
 
         @pl.when((k >= 2) & (k <= depth + 1))
         def _():
@@ -356,6 +367,17 @@
         return carry
 
     lax.fori_loop(0, depth, drain, 0)
+
+
+def place(ahead, back, out_ahead, out_back, sem):
+    copies = [
+        pltpu.make_async_copy(ahead, out_ahead, sem.at[0]),
+        pltpu.make_async_copy(back, out_back, sem.at[1]),
+    ]
+    for copy in copies:
+        copy.start()
+    for copy in copies:
+        copy.wait()
 
 
 def passed_along(block, axis, distance):
@@ -387,6 +409,7 @@
     ]
     vmem = pl.BlockSpec(memory_space=pltpu.VMEM)
     anywhere = pl.BlockSpec(memory_space=pl.ANY)
+    hbm = pl.BlockSpec(memory_space=pltpu.HBM)
     dma = pltpu.SemaphoreType.DMA
     ahead, back = pl.pallas_call(
         functools.partial(kernel, depth, experts, cap_f, cap_b),
@@ -430,6 +453,17 @@
         *tables, forward_input[0], backward_input[0], output_grad[0],
         weight_in[0, 0], weight_down[0, 0],
     )
+    if lax.axis_size("section") == 1:
+        ahead, back = pl.pallas_call(
+            place,
+            out_shape=(
+                jax.ShapeDtypeStruct((nf, width), BF),
+                jax.ShapeDtypeStruct((nb, width), BF),
+            ),
+            in_specs=[hbm] * 2,
+            out_specs=(hbm, hbm),
+            scratch_shapes=[dma((2,))],
+        )(ahead, back)
     forward_sent = passed_along(ahead[None], "section", 1)
     backward_sent = passed_along(back[None], "section", -1)
     return (forward_sent, backward_sent)

time: 84.3 us -> 91.2 us (1.082)
  Pallas kernels: 80.3 us -> 90.3 us
  local copies, waits for them, and re-layouts: 3.16 us -> 0 us
    pallas_call x0 -> x1, Pallas kernels: none -> 10.1 us  [on_device(): pl.pallas_call(place, out_shape=(jax.ShapeDtypeStruct((nf, width), BF), j...]
    unnamed x2 -> x0, local copies, waits for them, and re-layouts: 3.16 us -> none
where the time goes in v3:
time: 91.2 us; the launch traced here: 91 us
  Pallas kernels  90.3 us (99%)
    pallas_call x1, Pallas kernels, on_device(): pl.pallas_call(functools.partial(kernel, depth, experts, cap_f, cap_b), o...  80.3 us
    pallas_call x1, Pallas kernels, on_device(): pl.pallas_call(place, out_shape=(jax.ShapeDtypeStruct((nf, width), BF), j...  10.1 us

profile of v3, /device:TPU:24, one launch (start us, length us, event | category | flops | bytes accessed | tf_op | source)
XLA Modules:
  0.0 91.0 jit_solution(17875684265670451694)
XLA Ops:
  0.6 80.3 %shard_map.104 = (bf16[96,1024]{1,0:T(8,128)(2,1)}, bf16[48,1024]{1,0:T(8,128)(2,1)}) custom-call(s32[6,1,96]{2,1,0:T(1,128)} %bitcast.16, f32[6,1,96]{2,1,0:T(1,128)} %bitcast.17, s32[6,1,48]{2,1,0:T(1,128)} %bitcast.18, f32[6,1,48]{2,1,0:T(1,128)} %bitcast.19, bf16[96,1024]{1,0:T(8,128)(2,1)} %bitcast.13, bf16[48,1024]{1,0:T(8,128)(2,1)} %bitcast.14, ...), custom_call_target="tpu_custom_call" | custom-call | tf_op jit(solution)/shard_map/pallas_call | solution.py:414
  80.9 10.1 %shard_map.105 = (bf16[96,1024]{1,0:T(8,128)(2,1)}, bf16[48,1024]{1,0:T(8,128)(2,1)}) custom-call(bf16[96,1024]{1,0:T(8,128)(2,1)} %get-tuple-element.6.ahead, bf16[48,1024]{1,0:T(8,128)(2,1)} %get-tuple-element.7.back), custom_call_target="tpu_custom_call" | custom-call | tf_op jit(solution)/shard_map/pallas_call | solution.py:457

commit v4 on v2

--- a/solution.py
+++ b/solution.py
@@ -37,15 +37,18 @@
     depth, experts, cap_f, cap_b,
     routes_f, gates_f, routes_b, gates_b, tok_f, tok_b, grad_b, w_in, w_down,
     out_f, out_b,
-    blocks, send_d, recv_d, send_r, recv_r, send_p, recv_p, mine, acc_f, acc_b, own_f, own_b, wi, wd,
-    sem_load, sem_ws, sem_wr, sem_gs, sem_gr, sem_ds, sem_dr, sem_rs, sem_rr, sem_ps, sem_pr,
+    blocks, send_d, recv_d, send_t, recv_t, send_r, recv_r, send_p, recv_p,
+    mine, acc, own_f, own_b, wi, wd, order, packing,
+    sem_load, sem_ws, sem_wr, sem_gs, sem_gr, sem_ds, sem_dr, sem_ts, sem_tr, sem_rs, sem_rr, sem_ps, sem_pr,
 ):
     nf, width = tok_f.shape
     nb = tok_b.shape[0]
     half = w_down.shape[0]
-    rf = up16(cap_f)
-    rp = up16(2 * cap_b)
-    rb = up16(cap_b)
+    whole = (cap_f + 2 * cap_b) // 16 * 16
+    rest = cap_f + 2 * cap_b - whole
+    folds = width // 128
+    rt = folds * rest
+    mf, mb = up16(PLANE * cap_f), up16(PLANE * cap_b)
     rr = up16(cap_f + cap_b)
     sec = lax.axis_index("section")
     me = lax.axis_index("expert")
@@ -78,6 +81,8 @@
             barrier, inc=1, device_id=dev((z + q) % depth, p, c), device_id_type=MESH
         )
 
+    for load in loads[:3]:
+        load.wait()
     lanes = 256
     blocks[z, 0:experts, :] = jnp.zeros((experts, width), BF)
     for routes, gates, lane in ((routes_f, gates_f, 0), (routes_b, gates_b, 128)):
@@ -98,8 +103,6 @@
             start = part * lanes + lane
             blocks[z, 0:experts, start : start + count] = values
 
-    pl.semaphore_wait(barrier, 1 + (PLANE - 1) + (depth - 1))
-
     weight_copies = [
         pltpu.make_async_remote_copy(
             w_in, wi.at[c], sem_ws.at[0], sem_wr.at[0], device_id=dev(z, p, 1 - c), device_id_type=MESH
@@ -108,9 +111,6 @@
             w_down, wd.at[c], sem_ws.at[1], sem_wr.at[1], device_id=dev(z, p, 1 - c), device_id_type=MESH
         ),
     ]
-    for load in loads[:3]:
-        load.wait()
-
     def source(k):
         near = jnp.minimum(z, depth - 1 - z)
         side = jnp.where(k % 2 == 1, z - (k + 1) // 2, z + k // 2)
@@ -128,6 +128,9 @@
 
     def goes_left(zs):
         return (zs >= z) & (z > 0)
+
+    def passes_through(zs):
+        return (zs != z) & (goes_right(zs) | goes_left(zs))
 
     def send_on(zs):
         @pl.when(goes_right(zs))
@@ -188,48 +191,96 @@
     def slot(total, rows, count):
         return (iota((total, count), 0) % rows).astype(F32)
 
+    def tail_copy(zs, q):
+        tgt = (p + q) % PLANE
+        return pltpu.make_async_remote_copy(
+            send_t.at[zs, tgt], recv_t.at[zs, p], sem_ts.at[zs, q], sem_tr.at[zs, p],
+            device_id=dev(z, tgt, c), device_id_type=MESH,
+        )
+
+    def tail_arrival(zs, q):
+        other = (p + q) % PLANE
+        return pltpu.make_async_remote_copy(
+            send_t.at[zs, other], recv_t.at[zs, other], sem_ts.at[zs, q], sem_tr.at[zs, other],
+            device_id=dev(z, other, c), device_id_type=MESH,
+        )
+
+    def one_hot(hit):
+        return jnp.where(hit, 1.0, 0.0).astype(BF)
+
     def select(zs):
-        table_f = spread(zs, rf)[:, 0:nf]
-        pick_f = jnp.where(table_f == slot(PLANE * rf, rf, nf), 1.0, 0.0).astype(BF)
-        rows_f = dot(pick_f, blocks[zs, row_f : row_f + nf, :]).astype(BF)
-        table_b = spread(zs, rp)[:, 128 : 128 + nb]
-        place = slot(PLANE * rp, rp, nb)
-        pick_x = jnp.where(table_b == place, 1.0, 0.0).astype(BF)
-        pick_g = jnp.where(table_b + cap_b == place, 1.0, 0.0).astype(BF)
-        rows_b = (
-            dot(pick_x, blocks[zs, row_b : row_b + nb, :])
-            + dot(pick_g, blocks[zs, row_g : row_g + nb, :])
+        table = spread(zs, whole)
+        table_f, table_b = table[:, 0:nf], table[:, 128 : 128 + nb]
+        place_f, place_b = slot(PLANE * whole, whole, nf), slot(PLANE * whole, whole, nb)
+        x = blocks[zs, row_b : row_b + nb, :]
+        g = blocks[zs, row_g : row_g + nb, :]
+        rows = (
+            dot(one_hot(table_f == place_f), blocks[zs, row_f : row_f + nf, :])
+            + dot(one_hot(table_b + cap_f == place_b), x)
+            + dot(one_hot(table_b + (cap_f + cap_b) == place_b), g)
         ).astype(BF)
+        table_t = spread(zs, rt)[:, 128 : 128 + nb]
+        place_t = (iota((PLANE * rt, nb), 0) % rest + whole).astype(F32)
+        wide = dot(one_hot(table_t + (cap_f + cap_b) == place_t), g)
+        fold = iota((PLANE * rt, 128), 0) % rt // rest
+        tail = jnp.zeros((PLANE * rt, 128), F32)
+        for q in range(folds):
+            tail = tail + jnp.where(fold == q, wide[:, q * 128 : (q + 1) * 128], 0.0)
+        tail = tail.astype(BF)
         for q in range(PLANE):
-            send_d[zs, q, 0:rf, :] = rows_f[q * rf : (q + 1) * rf]
-            send_d[zs, q, rf : rf + rp, :] = rows_b[q * rp : (q + 1) * rp]
+            send_d[zs, q] = rows[q * whole : (q + 1) * whole]
+            send_t[zs, q] = tail[q * rt : (q + 1) * rt]
+
+    def dispatch(zs):
         for q in range(1, PLANE):
             dispatch_copy(zs, q).start()
+            tail_copy(zs, q).start()
         recv_d[zs, p] = send_d[zs, p]
-
-    def pack(rows, start, count):
-        row, col = iota((PLANE * rr, PLANE * rows), 0), iota((PLANE * rr, PLANE * rows), 1)
-        place = row % rr - start
-        hit = (row // rr == col // rows) & (place == col % rows) & (place >= 0) & (place < count)
-        return jnp.where(hit, 1.0, 0.0).astype(BF)
-
-    def expert(zs):
+        recv_t[zs, p] = send_t[zs, p]
+
+    def arrange():
+        for start, size, count, first in (
+            (0, mf, cap_f, 0), (mf, mb, cap_b, cap_f), (mf + mb, mb, cap_b, cap_f + cap_b)
+        ):
+            row, col = iota((size, PLANE * whole), 0), iota((size, PLANE * whole), 1)
+            hit = (row // count == col // whole) & (row % count + first == col % whole)
+            order[start : start + size] = one_hot(hit)
+        for start, size, count, first in ((0, mf, cap_f, 0), (mf, mb, cap_b, cap_f)):
+            shape = (PLANE * rr, size)
+            row, col = iota(shape, 0), iota(shape, 1)
+            hit = (row // rr == col // count) & (row % rr == col % count + first)
+            packing[:, start : start + size] = one_hot(hit)
+
+    def expert(zs, is_first):
         for q in range(1, PLANE):
             dispatch_arrival(zs, q).wait_recv()
-        got = recv_d[zs]
-        rows_f = got[:, 0:rf, :].reshape(PLANE * rf, width)
-        rows_b = got[:, rf : rf + rp, :].reshape(PLANE * rp, width)
-        shape = (PLANE * rb, PLANE * rp)
-        row, col = iota(shape, 0), iota(shape, 1)
-        same = (row // rb == col // rp) & (row % rb < cap_b)
-        rows_x = dot(jnp.where(same & (col % rp == row % rb), 1.0, 0.0).astype(BF), rows_b)
-        rows_g = dot(jnp.where(same & (col % rp == row % rb + cap_b), 1.0, 0.0).astype(BF), rows_b)
-        mf, mb = PLANE * rf, PLANE * rb
-        mine[0:mf] = rows_f
-        mine[mf : mf + mb] = rows_x.astype(BF)
-        mine[mf + mb : mf + 2 * mb] = rows_g.astype(BF)
-
-        def one_half(h, carry):
+            tail_arrival(zs, q).wait_recv()
+        rows = dot(order[...], recv_d[zs].reshape(PLANE * whole, width))
+        tail = recv_t[zs].reshape(PLANE * rt, 128)
+        fold = iota((PLANE * rt, 128), 0) % rt // rest
+        wide = jnp.concatenate(
+            [jnp.where(fold == q, tail, jnp.zeros_like(tail)) for q in range(folds)], axis=1
+        )
+        row, col = iota((mb, PLANE * rt), 0), iota((mb, PLANE * rt), 1)
+        hit = (row // cap_b == col // rt) & (
+            row % cap_b + (cap_f + cap_b) == col % rest + whole
+        )
+        mine[0 : mf + mb] = rows[0 : mf + mb].astype(BF)
+        mine[mf + mb :] = (rows[mf + mb :] + dot(one_hot(hit), wide)).astype(BF)
+
+        def one_half(i, carry):
+            h = (c + i) % 2
+
+            @pl.when(is_first & (i == 0))
+            def _():
+                for load in loads[3:]:
+                    load.wait()
+
+            @pl.when(is_first & (i == 1))
+            def _():
+                for copy in weight_copies:
+                    copy.wait_recv()
+
             hidden = dot(mine[0 : mf + mb], wi[h])
             a, b = hidden[:, :half], hidden[:, half:]
             q = jax.nn.sigmoid(a)
@@ -240,23 +291,22 @@
             grad = jnp.concatenate([u * b * q * (1.0 + a * (1.0 - q)), u * a * q], axis=1)
             part_b = dot_t(grad.astype(BF), wi[h])
 
-            @pl.when(h == 0)
+            @pl.when(i == 0)
             def _():
-                acc_f[...] = part_f
-                acc_b[...] = part_b
-
-            @pl.when(h == 1)
+                acc[0:mf] = part_f
+                acc[mf : mf + mb] = part_b
+
+            @pl.when(i == 1)
             def _():
-                total_f = (acc_f[...] + part_f).astype(BF)
-                total_b = (acc_b[...] + part_b).astype(BF)
-                packed = dot(pack(rf, 0, cap_f), total_f) + dot(pack(rb, cap_f, cap_b), total_b)
-                packed = packed.astype(BF)
-                for j in range(PLANE):
-                    send_r[zs, j] = packed[j * rr : (j + 1) * rr]
+                acc[0:mf] = acc[0:mf] + part_f
+                acc[mf : mf + mb] = acc[mf : mf + mb] + part_b
 
             return carry
 
         lax.fori_loop(0, 2, one_half, 0)
+        packed = dot(packing[...], acc[...].astype(BF)).astype(BF)
+        for j in range(PLANE):
+            send_r[zs, j] = packed[j * rr : (j + 1) * rr]
         for q in range(1, PLANE):
             return_copy(zs, q).start()
         recv_r[zs, p] = send_r[zs, p]
@@ -286,34 +336,31 @@
             send_p[zs, nf : nf + nb, :] = part_b.astype(BF)
             part_copy(zs).start()
 
+    def pass_on(zs):
+        @pl.when(passes_through(zs))
+        def _():
+            relay(zs, 0).wait_recv()
+            send_on(zs)
+
     def step(k, carry):
         @pl.when(k < depth)
         def _():
             zs = source(k)
 
-            @pl.when(zs != z)
+            @pl.when(jnp.logical_not(passes_through(zs)))
             def _():
                 relay(zs, 0).wait_recv()
 
-            send_on(zs)
-
-            @pl.when(k == 0)
-            def _():
-                for copy in weight_copies:
-                    copy.start()
-
             select(zs)
+            dispatch(zs)
+
+        @pl.when(k < depth - 1)
+        def _():
+            pass_on(source(k + 1))
 
         @pl.when((k >= 2) & (k <= depth + 1))
         def _():
-            @pl.when(k == 2)
-            def _():
-                for load in loads[3:]:
-                    load.wait()
-                for copy in weight_copies:
-                    copy.wait_recv()
-
-            expert(source((k - 1) % depth))
+            expert(source((k - 1) % depth), k == 2)
 
         @pl.when(k >= 3)
         def _():
@@ -321,7 +368,15 @@
 
         return carry
 
-    lax.fori_loop(0, depth + 3, step, 0)
+    select(z)
+    pl.semaphore_wait(barrier, 1 + (PLANE - 1) + (depth - 1))
+    send_on(z)
+    dispatch(z)
+    for copy in weight_copies:
+        copy.start()
+    arrange()
+    pass_on(source(1))
+    lax.fori_loop(1, depth + 3, step, 0)
 
     total_f = blocks[z, row_f : row_f + nf, :].astype(F32)
     total_b = blocks[z, row_g : row_g + nb, :].astype(F32)
@@ -347,6 +402,7 @@
 
         for q in range(1, PLANE):
             dispatch_copy(zs, q).wait_send()
+            tail_copy(zs, q).wait_send()
             return_copy(zs, q).wait_send()
 
         @pl.when(zs != z)
@@ -379,7 +435,9 @@
     half = weight_down.shape[2]
     cap_f = 2 * (7 * nf // (2 * experts))
     cap_b = 2 * (7 * nb // (2 * experts))
-    rf, rp, rb = up16(cap_f), up16(2 * cap_b), up16(cap_b)
+    whole = (cap_f + 2 * cap_b) // 16 * 16
+    rt = (cap_f + 2 * cap_b - whole) * (width // 128)
+    mf, mb = up16(PLANE * cap_f), up16(PLANE * cap_b)
     rr = up16(cap_f + cap_b)
     tables = [
         jnp.transpose(array, (2, 0, 1))
@@ -398,24 +456,29 @@
         out_specs=(vmem, vmem),
         scratch_shapes=[
             pltpu.VMEM((depth, experts + 2 * nb + nf, width), BF),
-            pltpu.VMEM((depth, PLANE, rf + rp, width), BF),
-            pltpu.VMEM((depth, PLANE, rf + rp, width), BF),
+            pltpu.VMEM((depth, PLANE, whole, width), BF),
+            pltpu.VMEM((depth, PLANE, whole, width), BF),
+            pltpu.VMEM((depth, PLANE, rt, 128), BF),
+            pltpu.VMEM((depth, PLANE, rt, 128), BF),
             pltpu.VMEM((depth, PLANE, rr, width), BF),
             pltpu.VMEM((depth, PLANE, rr, width), BF),
             pltpu.VMEM((depth, nf + nb, width), BF),
             pltpu.VMEM((depth, nf + nb, width), BF),
-            pltpu.VMEM((PLANE * (rf + 2 * rb), width), BF),
-            pltpu.VMEM((PLANE * rf, width), F32),
-            pltpu.VMEM((PLANE * rb, width), F32),
+            pltpu.VMEM((mf + 2 * mb, width), BF),
+            pltpu.VMEM((mf + mb, width), F32),
             pltpu.VMEM((nf, width), F32),
             pltpu.VMEM((nb, width), F32),
             pltpu.VMEM((2, width, 2 * half), BF),
             pltpu.VMEM((2, half, width), BF),
+            pltpu.VMEM((mf + 2 * mb, PLANE * whole), BF),
+            pltpu.VMEM((PLANE * rr, mf + mb), BF),
             dma((5,)),
             dma((2,)),
             dma((2,)),
             dma((depth, 2)),
             dma((depth,)),
+            dma((depth, PLANE)),
+            dma((depth, PLANE)),
             dma((depth, PLANE)),
             dma((depth, PLANE)),
             dma((depth, PLANE)),

time: 84.3 us -> 81.3 us (0.964)
  Pallas kernels: 80.3 us -> 77.3 us
    pallas_call x1, Pallas kernels: 80.3 us -> 77.3 us  [on_device(): pl.pallas_call(functools.partial(kernel, depth, experts, cap_f, cap_b), o...]
where the time goes in v4:
time: 81.3 us; the launch traced here: 81.1 us
  Pallas kernels  77.3 us (95%)
  local copies, waits for them, and re-layouts  3.16 us (4%)
    pallas_call x1, Pallas kernels, on_device(): pl.pallas_call(functools.partial(kernel, depth, experts, cap_f, cap_b), o...  77.3 us
    unnamed x2, local copies, waits for them, and re-layouts  3.16 us

profile of v4, /device:TPU:24, one launch (start us, length us, event | category | flops | bytes accessed | tf_op | source)
XLA Modules:
  0.0 81.1 jit_solution(12853594351179553348)
XLA Ops:
  0.6 77.3 %shard_map.104 = (bf16[96,1024]{1,0:T(8,128)(2,1)}, bf16[48,1024]{1,0:T(8,128)(2,1)}) custom-call(s32[6,1,96]{2,1,0:T(1,128)} %bitcast.18, f32[6,1,96]{2,1,0:T(1,128)} %bitcast.19, s32[6,1,48]{2,1,0:T(1,128)} %bitcast.20, f32[6,1,48]{2,1,0:T(1,128)} %bitcast.21, bf16[96,1024]{1,0:T(8,128)(2,1)} %bitcast.14, bf16[48,1024]{1,0:T(8,128)(2,1)} %bitcast.15, ...), custom_call_target="tpu_custom_call" | custom-call | tf_op jit(solution)/shard_map/pallas_call | solution.py:449
  77.9 1.6 %copy.13 = bf16[1,96,1024]{2,1,0:T(8,128)(2,1)} copy(bf16[1,96,1024]{2,1,0:T(8,128)(2,1)} %bitcast.13) | data formatting | bytes 393216
  79.5 1.5 %copy.14 = bf16[1,48,1024]{2,1,0:T(8,128)(2,1)} copy(bf16[1,48,1024]{2,1,0:T(8,128)(2,1)} %bitcast.17) | data formatting | bytes 196608

commit v5 on v4

--- a/solution.py
+++ b/solution.py
@@ -358,13 +358,13 @@
         def _():
             pass_on(source(k + 1))
 
-        @pl.when((k >= 2) & (k <= depth + 1))
-        def _():
-            expert(source((k - 1) % depth), k == 2)
-
         @pl.when(k >= 3)
         def _():
-            combine(source((k - 2) % depth))
+            combine(source(k - 3))
+
+        @pl.when(k <= depth)
+        def _():
+            expert(source(k - 1), k == 1)
 
         return carry
 

time: 81.3 us -> 86.8 us (1.068)
  Pallas kernels: 77.3 us -> 82.8 us
    pallas_call x1, Pallas kernels: 77.3 us -> 82.8 us  [on_device(): pl.pallas_call(functools.partial(kernel, depth, experts, cap_f, cap_b), o...]
where the time goes in v5:
time: 86.8 us; the launch traced here: 86.6 us
  Pallas kernels  82.8 us (95%)
  local copies, waits for them, and re-layouts  3.16 us (4%)
    pallas_call x1, Pallas kernels, on_device(): pl.pallas_call(functools.partial(kernel, depth, experts, cap_f, cap_b), o...  82.8 us
    unnamed x2, local copies, waits for them, and re-layouts  3.16 us

profile of v5, /device:TPU:24, one launch (start us, length us, event | category | flops | bytes accessed | tf_op | source)
XLA Modules:
  0.0 86.6 jit_solution(3997141508584113179)
XLA Ops:
  0.6 82.8 %shard_map.104 = (bf16[96,1024]{1,0:T(8,128)(2,1)}, bf16[48,1024]{1,0:T(8,128)(2,1)}) custom-call(s32[6,1,96]{2,1,0:T(1,128)} %bitcast.18, f32[6,1,96]{2,1,0:T(1,128)} %bitcast.19, s32[6,1,48]{2,1,0:T(1,128)} %bitcast.20, f32[6,1,48]{2,1,0:T(1,128)} %bitcast.21, bf16[96,1024]{1,0:T(8,128)(2,1)} %bitcast.14, bf16[48,1024]{1,0:T(8,128)(2,1)} %bitcast.15, ...), custom_call_target="tpu_custom_call" | custom-call | tf_op jit(solution)/shard_map/pallas_call | solution.py:449
  83.5 1.6 %copy.13 = bf16[1,96,1024]{2,1,0:T(8,128)(2,1)} copy(bf16[1,96,1024]{2,1,0:T(8,128)(2,1)} %bitcast.13) | data formatting | bytes 393216
  85.1 1.5 %copy.14 = bf16[1,48,1024]{2,1,0:T(8,128)(2,1)} copy(bf16[1,48,1024]{2,1,0:T(8,128)(2,1)} %bitcast.17) | data formatting | bytes 196608

commit v6 on v4

--- a/solution.py
+++ b/solution.py
@@ -105,10 +105,10 @@
 
     weight_copies = [
         pltpu.make_async_remote_copy(
-            w_in, wi.at[c], sem_ws.at[0], sem_wr.at[0], device_id=dev(z, p, 1 - c), device_id_type=MESH
+            wi.at[c], wi.at[c], sem_ws.at[0], sem_wr.at[0], device_id=dev(z, p, 1 - c), device_id_type=MESH
         ),
         pltpu.make_async_remote_copy(
-            w_down, wd.at[c], sem_ws.at[1], sem_wr.at[1], device_id=dev(z, p, 1 - c), device_id_type=MESH
+            wd.at[c], wd.at[c], sem_ws.at[1], sem_wr.at[1], device_id=dev(z, p, 1 - c), device_id_type=MESH
         ),
     ]
     def source(k):
@@ -271,11 +271,6 @@
         def one_half(i, carry):
             h = (c + i) % 2
 
-            @pl.when(is_first & (i == 0))
-            def _():
-                for load in loads[3:]:
-                    load.wait()
-
             @pl.when(is_first & (i == 1))
             def _():
                 for copy in weight_copies:
@@ -372,7 +367,8 @@
     pl.semaphore_wait(barrier, 1 + (PLANE - 1) + (depth - 1))
     send_on(z)
     dispatch(z)
-    for copy in weight_copies:
+    for load, copy in zip(loads[3:], weight_copies):
+        load.wait()
         copy.start()
     arrange()
     pass_on(source(1))

time: 81.3 us -> 81.1 us (level)
  no operation moved by 1% of the time
where the time goes in v6:
time: 81.1 us; the launch traced here: 80.9 us
  Pallas kernels  77.2 us (95%)
  local copies, waits for them, and re-layouts  3.16 us (4%)
    pallas_call x1, Pallas kernels, on_device(): pl.pallas_call(functools.partial(kernel, depth, experts, cap_f, cap_b), o...  77.2 us
    unnamed x2, local copies, waits for them, and re-layouts  3.16 us

profile of v6, /device:TPU:24, one launch (start us, length us, event | category | flops | bytes accessed | tf_op | source)
XLA Modules:
  0.0 80.9 jit_solution(6006954247594798693)
XLA Ops:
  0.6 77.2 %shard_map.104 = (bf16[96,1024]{1,0:T(8,128)(2,1)}, bf16[48,1024]{1,0:T(8,128)(2,1)}) custom-call(s32[6,1,96]{2,1,0:T(1,128)} %bitcast.18, f32[6,1,96]{2,1,0:T(1,128)} %bitcast.19, s32[6,1,48]{2,1,0:T(1,128)} %bitcast.20, f32[6,1,48]{2,1,0:T(1,128)} %bitcast.21, bf16[96,1024]{1,0:T(8,128)(2,1)} %bitcast.14, bf16[48,1024]{1,0:T(8,128)(2,1)} %bitcast.15, ...), custom_call_target="tpu_custom_call" | custom-call | tf_op jit(solution)/shard_map/pallas_call | solution.py:445
  77.8 1.6 %copy.13 = bf16[1,96,1024]{2,1,0:T(8,128)(2,1)} copy(bf16[1,96,1024]{2,1,0:T(8,128)(2,1)} %bitcast.13) | data formatting | bytes 393216
  79.4 1.5 %copy.14 = bf16[1,48,1024]{2,1,0:T(8,128)(2,1)} copy(bf16[1,48,1024]{2,1,0:T(8,128)(2,1)} %bitcast.17) | data formatting | bytes 196608

commit v7 on v6

--- a/solution.py
+++ b/solution.py
@@ -251,7 +251,7 @@
             hit = (row // rr == col // count) & (row % rr == col % count + first)
             packing[:, start : start + size] = one_hot(hit)
 
-    def expert(zs, is_first):
+    def gather_rows(zs):
         for q in range(1, PLANE):
             dispatch_arrival(zs, q).wait_recv()
             tail_arrival(zs, q).wait_recv()
@@ -265,41 +265,32 @@
         hit = (row // cap_b == col // rt) & (
             row % cap_b + (cap_f + cap_b) == col % rest + whole
         )
-        mine[0 : mf + mb] = rows[0 : mf + mb].astype(BF)
-        mine[mf + mb :] = (rows[mf + mb :] + dot(one_hot(hit), wide)).astype(BF)
-
-        def one_half(i, carry):
-            h = (c + i) % 2
-
-            @pl.when(is_first & (i == 1))
-            def _():
-                for copy in weight_copies:
-                    copy.wait_recv()
-
-            hidden = dot(mine[0 : mf + mb], wi[h])
-            a, b = hidden[:, :half], hidden[:, half:]
-            q = jax.nn.sigmoid(a)
-            active = (a[:mf] * q[:mf] * b[:mf]).astype(BF)
-            part_f = dot(active, wd[h])
-            u = dot_t(mine[mf + mb : mf + 2 * mb], wd[h])
-            a, b, q = a[mf:], b[mf:], q[mf:]
-            grad = jnp.concatenate([u * b * q * (1.0 + a * (1.0 - q)), u * a * q], axis=1)
-            part_b = dot_t(grad.astype(BF), wi[h])
-
-            @pl.when(i == 0)
-            def _():
-                acc[0:mf] = part_f
-                acc[mf : mf + mb] = part_b
-
-            @pl.when(i == 1)
-            def _():
-                acc[0:mf] = acc[0:mf] + part_f
-                acc[mf : mf + mb] = acc[mf : mf + mb] + part_b
-
-            return carry
-
-        lax.fori_loop(0, 2, one_half, 0)
-        packed = dot(packing[...], acc[...].astype(BF)).astype(BF)
+        mine[zs, 0 : mf + mb] = rows[0 : mf + mb].astype(BF)
+        mine[zs, mf + mb :] = (rows[mf + mb :] + dot(one_hot(hit), wide)).astype(BF)
+
+    def work(zs, h):
+        hidden = dot(mine[zs, 0 : mf + mb], wi[h])
+        a, b = hidden[:, :half], hidden[:, half:]
+        q = jax.nn.sigmoid(a)
+        active = (a[:mf] * q[:mf] * b[:mf]).astype(BF)
+        part_f = dot(active, wd[h])
+        u = dot_t(mine[zs, mf + mb : mf + 2 * mb], wd[h])
+        a, b, q = a[mf:], b[mf:], q[mf:]
+        grad = jnp.concatenate([u * b * q * (1.0 + a * (1.0 - q)), u * a * q], axis=1)
+        part_b = dot_t(grad.astype(BF), wi[h])
+        return part_f, part_b
+
+    def own_half(zs):
+        gather_rows(zs)
+        part_f, part_b = work(zs, c)
+        acc[zs, 0:mf] = part_f
+        acc[zs, mf : mf + mb] = part_b
+
+    def other_half(zs):
+        part_f, part_b = work(zs, 1 - c)
+        acc[zs, 0:mf] = acc[zs, 0:mf] + part_f
+        acc[zs, mf : mf + mb] = acc[zs, mf : mf + mb] + part_b
+        packed = dot(packing[...], acc[zs].astype(BF)).astype(BF)
         for j in range(PLANE):
             send_r[zs, j] = packed[j * rr : (j + 1) * rr]
         for q in range(1, PLANE):
@@ -353,13 +344,22 @@
         def _():
             pass_on(source(k + 1))
 
-        @pl.when((k >= 2) & (k <= depth + 1))
-        def _():
-            expert(source((k - 1) % depth), k == 2)
-
-        @pl.when(k >= 3)
-        def _():
-            combine(source((k - 2) % depth))
+        @pl.when(k == 3)
+        def _():
+            for copy in weight_copies:
+                copy.wait_recv()
+
+        @pl.when((k >= 3) & (k <= depth + 2))
+        def _():
+            other_half(source((k - 2) % depth))
+
+        @pl.when(k >= 4)
+        def _():
+            combine(source((k - 3) % depth))
+
+        @pl.when(k <= depth)
+        def _():
+            own_half(source(k - 1))
 
         return carry
 
@@ -372,7 +372,7 @@
         copy.start()
     arrange()
     pass_on(source(1))
-    lax.fori_loop(1, depth + 3, step, 0)
+    lax.fori_loop(1, depth + 4, step, 0)
 
     total_f = blocks[z, row_f : row_f + nf, :].astype(F32)
     total_b = blocks[z, row_g : row_g + nb, :].astype(F32)
@@ -460,8 +460,8 @@
             pltpu.VMEM((depth, PLANE, rr, width), BF),
             pltpu.VMEM((depth, nf + nb, width), BF),
             pltpu.VMEM((depth, nf + nb, width), BF),
-            pltpu.VMEM((mf + 2 * mb, width), BF),
-            pltpu.VMEM((mf + mb, width), F32),
+            pltpu.VMEM((depth, mf + 2 * mb, width), BF),
+            pltpu.VMEM((depth, mf + mb, width), F32),
             pltpu.VMEM((nf, width), F32),
             pltpu.VMEM((nb, width), F32),
             pltpu.VMEM((2, width, 2 * half), BF),

time: 81.1 us -> 82.5 us (1.017)
  Pallas kernels: 77.2 us -> 78.5 us
    pallas_call x1, Pallas kernels: 77.2 us -> 78.5 us  [on_device(): pl.pallas_call(functools.partial(kernel, depth, experts, cap_f, cap_b), o...]
where the time goes in v7:
time: 82.5 us; the launch traced here: 82.3 us
  Pallas kernels  78.5 us (95%)
  local copies, waits for them, and re-layouts  3.16 us (4%)
    pallas_call x1, Pallas kernels, on_device(): pl.pallas_call(functools.partial(kernel, depth, experts, cap_f, cap_b), o...  78.5 us
    unnamed x2, local copies, waits for them, and re-layouts  3.16 us

profile of v7, /device:TPU:24, one launch (start us, length us, event | category | flops | bytes accessed | tf_op | source)
XLA Modules:
  0.0 82.3 jit_solution(15192104796322664691)
XLA Ops:
  0.6 78.5 %shard_map.104 = (bf16[96,1024]{1,0:T(8,128)(2,1)}, bf16[48,1024]{1,0:T(8,128)(2,1)}) custom-call(s32[6,1,96]{2,1,0:T(1,128)} %bitcast.18, f32[6,1,96]{2,1,0:T(1,128)} %bitcast.19, s32[6,1,48]{2,1,0:T(1,128)} %bitcast.20, f32[6,1,48]{2,1,0:T(1,128)} %bitcast.21, bf16[96,1024]{1,0:T(8,128)(2,1)} %bitcast.14, bf16[48,1024]{1,0:T(8,128)(2,1)} %bitcast.15, ...), custom_call_target="tpu_custom_call" | custom-call | tf_op jit(solution)/shard_map/pallas_call | solution.py:445
  79.1 1.6 %copy.13 = bf16[1,96,1024]{2,1,0:T(8,128)(2,1)} copy(bf16[1,96,1024]{2,1,0:T(8,128)(2,1)} %bitcast.13) | data formatting | bytes 393216
  80.8 1.5 %copy.14 = bf16[1,48,1024]{2,1,0:T(8,128)(2,1)} copy(bf16[1,48,1024]{2,1,0:T(8,128)(2,1)} %bitcast.17) | data formatting | bytes 196608
